TPU v7x, 128 devices: a whole 4x4x4 slice. The times are simulated.
128 devices in a mesh: row: 8 (over y, core), col: 16 (over x, z).
Axes of the slice: x: 4, y: 4, z: 4, core: 2. Of those that a mesh axis runs over, the one named last changes fastest.
Arguments:
- covariance: float32 [4, 4096, 2, 8192], P(None, 'row', None, 'col'), may hold values from 0 to 2, as said below
- band_mask: int32 [32, 32], replicated, may hold values from 0 to 1, as said below
Outputs:
- schur: float32 [4, 4096, 2, 8192], P(None, 'row', None, 'col')
- panels: float32 [4, 4096, 1024], P(None, 'row')
Inputs may be any that keep to these rules, and one draw needn't show every extreme that they name: band_mask is symmetric, holds 0 or 1, and is 1 wherever the two tile indices differ by at most 1 and wherever either tile index is below 2. covariance is symmetric, with 1 added on its diagonal; A is positive definite.
All inputs are finite; a program needn't handle non-finite values.
Results may differ from a plain program's by a relative error of at most 0.0003.
Values sent between devices are 32-bit elements; how exact they have to be, the bound alone decides.
A program may use at most 128 MiB of HBM per device.

v0:
```python
import jax
import jax.numpy as jnp
from jax import lax
from jax.sharding import PartitionSpec as P

TILE = 512


def from_root(value, axis, root):
    mine = lax.axis_index(axis) == root
    return lax.psum(jnp.where(mine, value, jnp.zeros_like(value)), axis)


def solve_below(factor, column, tile_ids, index):
    count = column.shape[0]
    rhs_block = jnp.transpose(column, (2, 0, 1)).reshape(TILE, count * TILE)
    solved = lax.linalg.triangular_solve(factor, rhs_block, left_side=True, lower=True)
    solved = jnp.transpose(solved.reshape(TILE, count, TILE), (1, 2, 0))
    chosen = tile_ids[:, None, None]
    return jnp.where(
        chosen > index, solved, jnp.where(chosen == index, factor[None], jnp.zeros_like(solved))
    )


def outer_update(target, row_part, col_part):
    return target - jnp.einsum("mab,ncb->manc", row_part, col_part, precision=lax.Precision.HIGHEST)


def body(covariance, band_mask):
    row_count = lax.axis_size("row")
    col_count = lax.axis_size("col")
    row_index = lax.axis_index("row")
    col_index = lax.axis_index("col")
    tile_total = band_mask.shape[0]
    row_tiles = tile_total // row_count
    col_tiles = tile_total // col_count
    row_ids = jnp.arange(row_tiles, dtype=jnp.int32) * row_count + row_index
    col_ids = jnp.arange(col_tiles, dtype=jnp.int32) * col_count + col_index
    keep_all = band_mask.astype(jnp.float32)
    keep_rows = lax.dynamic_index_in_dim(
        keep_all.reshape(row_tiles, row_count, tile_total), row_index, 1, keepdims=False
    )
    keep_local = lax.dynamic_index_in_dim(
        keep_rows.reshape(row_tiles, col_tiles, col_count), col_index, 2, keepdims=False
    )
    schur = covariance * keep_local[:, None, :, None]

    def to_columns(row_part):
        grouped = row_part.reshape(col_tiles, col_count // row_count, TILE, TILE)
        picked = lax.dynamic_index_in_dim(grouped, col_index // row_count, 1, keepdims=False)
        return from_root(picked, "row", col_index % row_count)

    def make_panel(column, column_step):
        diag_local = column[column_step // row_count]
        received = from_root(diag_local, "row", column_step % row_count)
        identity = jnp.eye(TILE, dtype=jnp.float32)
        diagonal = jnp.where(col_index == column_step % col_count, received, identity)
        factor = jnp.linalg.cholesky(diagonal)
        panel = solve_below(factor, column, row_ids, column_step)
        row_part = from_root(panel, "col", column_step % col_count)
        return (row_part, to_columns(row_part))

    rows_zero, cols_zero = make_panel(schur[:, :, 0, :], 0)
    schur = outer_update(schur, rows_zero, cols_zero)
    rows_one, cols_one = make_panel(schur[:, :, 0, :], 1)
    schur = outer_update(schur, rows_one, cols_one)
    row_keep = (row_ids >= 2).astype(jnp.float32)
    col_keep = (col_ids >= 2).astype(jnp.float32)
    schur = schur * row_keep[:, None, None, None] * col_keep[None, None, :, None]
    panels = jnp.concatenate([rows_zero, rows_one], axis=2)
    return (schur, panels)


def solution(mesh):
    return jax.shard_map(
        body,
        mesh=mesh,
        in_specs=(P(None, "row", None, "col"), P()),
        out_specs=(P(None, "row", None, "col"), P(None, "row", None)),
        check_vma=False,
    )
```

profile of v0, /device:TPU:0, one launch (start us, length us, event | category | flops | bytes accessed | tf_op | source)
XLA Modules:
  0.0 887.7 jit_solution(13052598460974647819)
XLA Ops:
  8.3 13.1 %copy.18 = f32[4,512,2,512]{1,3,2,0:T(8,128)} copy(f32[4,512,2,512]{3,2,1,0:T(2,128)} %param.5) | data formatting | bytes 16777216 | tf_op args[0]
  21.4 4.5 broadcast_multiply_fusion
  25.9 3.4 copy-done.1
  29.3 1.1 fusion.42
  30.5 4.6 slice_bitcast_fusion.1
  35.1 5.4 copy.20
  40.6 54.9 %all-reduce.8.cloned.1.call-done = f32[512,512]{0,1:T(8,128)} async-done(((f32[512,512]{0,1:T(8,128)}), f32[512,512]{0,1:T(8,128)}) %all-reduce.8.cloned.1.call-update) | async-done | bytes 1048592 | tf_op jit(solution)/shard_map/psum | solution.py:11
  95.5 1.4 convert_select_fusion.1
  97.6 11.7 %cholesky.286 = f32[128,128]{1,0:T(8,128)S(1)} custom-call(f32[128,128]{1,0:T(8,128)S(1)} %cholesky.426), custom_call_target="Cholesky" | custom-call | tf_op jit(solution)/shard_map/jit(cholesky)/cholesky | solution.py:58
  109.3 9.8 %custom-call.27 = f32[1,128,128]{1,2,0:T(8,128)S(1)} custom-call(f32[1,128,128]{2,1,0:T(8,128)S(1)} %get-tuple-element.67), custom_call_target="InvertDiagBlocksLowerTriangular" | custom-call | tf_op jit(solution)/shard_map/jit(cholesky)/cholesky | solution.py:58
  119.9 11.7 %cholesky.305 = f32[128,128]{1,0:T(8,128)S(1)} custom-call(f32[128,128]{1,0:T(8,128)S(1)} %cholesky.430), custom_call_target="Cholesky" | custom-call | tf_op jit(solution)/shard_map/jit(cholesky)/cholesky | solution.py:58
  131.7 10.2 %custom-call.28 = f32[1,128,128]{1,2,0:T(8,128)S(1)} custom-call(f32[1,128,128]{2,1,0:T(8,128)S(1)} %get-tuple-element.64), custom_call_target="InvertDiagBlocksLowerTriangular" | custom-call | tf_op jit(solution)/shard_map/jit(cholesky)/cholesky | solution.py:58
  142.6 11.7 %cholesky.326 = f32[128,128]{1,0:T(8,128)S(1)} custom-call(f32[128,128]{1,0:T(8,128)S(1)} %cholesky.435), custom_call_target="Cholesky" | custom-call | tf_op jit(solution)/shard_map/jit(cholesky)/cholesky | solution.py:58
  155.0 9.8 %custom-call.29 = f32[1,128,128]{1,2,0:T(8,128)S(1)} custom-call(f32[1,128,128]{2,1,0:T(8,128)S(1)} %get-tuple-element.61), custom_call_target="InvertDiagBlocksLowerTriangular" | custom-call | tf_op jit(solution)/shard_map/jit(cholesky)/cholesky | solution.py:58
  165.4 11.7 %cholesky.343 = f32[128,128]{1,0:T(8,128)S(1)} custom-call(f32[128,128]{1,0:T(8,128)S(1)} %convolution_subtract_fusion.9), custom_call_target="Cholesky" | custom-call | tf_op jit(solution)/shard_map/jit(cholesky)/cholesky | solution.py:58
  181.6 7.9 while.4
  182.2 1.4 bitcast_dynamic-update-slice_fusion.4
  184.2 1.4 bitcast_dynamic-update-slice_fusion.4
  186.1 1.4 bitcast_dynamic-update-slice_fusion.4
  188.1 1.4 bitcast_dynamic-update-slice_fusion.4
  189.5 39.3 %custom-call.30 = f32[4,128,128]{1,2,0:T(8,128)S(1)} custom-call(f32[4,128,128]{2,1,0:T(8,128)S(1)} %get-tuple-element.18), custom_call_target="InvertDiagBlocksLowerTriangular" | custom-call | tf_op jit(solution)/shard_map/triangular_solve/custom-call.3 | solution.py:17
  228.8 2.4 fusion.40
  231.2 3.0 convolution_subtract_fusion.3
  235.4 3.5 convolution_subtract_fusion.1
  238.9 1.1 fusion.71
  240.0 5.6 fusion.24
  246.6 2.5 pad_maximum_fusion.1
  249.2 5.3 copy.34
  254.5 4.9 select_select_fusion.1
  259.5 102.4 %all-reduce.10.cloned.1.call-done = f32[4,512,512]{2,1,0:T(8,128)} async-done(((f32[4,512,512]{2,1,0:T(8,128)}), f32[4,512,512]{2,1,0:T(8,128)}) %all-reduce.10.cloned.1.call-update) | async-done | bytes 4194320 | tf_op jit(solution)/shard_map/psum | solution.py:11
  362.0 3.1 fusion.34
  365.2 65.4 %all-reduce.12.cloned.1.call-done = f32[2,512,512]{2,1,0:T(8,128)} async-done(((f32[2,512,512]{2,1,0:T(8,128)}), f32[2,512,512]{2,1,0:T(8,128)}) %all-reduce.12.cloned.1.call-update) | async-done | bytes 2097168 | tf_op jit(solution)/shard_map/psum | solution.py:11
  430.6 16.9 %fusion.18 = f32[4,512,2,512]{1,3,2,0:T(8,128)S(1)} fusion(f32[4,512,2,512]{1,3,2,0:T(8,128)} %copy-done.1, f32[4,512,512]{2,1,0:T(8,128)} %all-reduce.10.cloned.1.call-done, f32[2,512,512]{2,1,0:T(8,128)} %all-reduce.12.cloned.1.call-done), kind=kOutput, calls=%fused_computation.29 | convolution fusion | flops 12886999040 | bytes 23068672 | tf_op jit(solution)/shard_map/mab,ncb->manc/dot_general | solution.py:26
  447.5 3.4 copy-done
  452.1 4.6 slice_bitcast_fusion
  456.7 5.6 copy.25
  462.4 51.8 %all-reduce.14.cloned.1.call-done = f32[512,512]{0,1:T(8,128)} async-done(((f32[512,512]{0,1:T(8,128)}), f32[512,512]{0,1:T(8,128)}) %all-reduce.14.cloned.1.call-update) | async-done | bytes 1048592 | tf_op jit(solution)/shard_map/psum | solution.py:11
  515.6 11.7 %cholesky.358 = f32[128,128]{1,0:T(8,128)S(1)} custom-call(f32[128,128]{1,0:T(8,128)S(1)} %cholesky.439), custom_call_target="Cholesky" | custom-call | tf_op jit(solution)/shard_map/jit(cholesky)/cholesky | solution.py:58
  528.0 9.8 %custom-call.31 = f32[1,128,128]{1,2,0:T(8,128)S(1)} custom-call(f32[1,128,128]{2,1,0:T(8,128)S(1)} %get-tuple-element.57), custom_call_target="InvertDiagBlocksLowerTriangular" | custom-call | tf_op jit(solution)/shard_map/jit(cholesky)/cholesky | solution.py:58
  538.6 11.7 %cholesky.377 = f32[128,128]{1,0:T(8,128)S(1)} custom-call(f32[128,128]{1,0:T(8,128)S(1)} %cholesky.443), custom_call_target="Cholesky" | custom-call | tf_op jit(solution)/shard_map/jit(cholesky)/cholesky | solution.py:58
  551.0 10.0 %custom-call.32 = f32[1,128,128]{1,2,0:T(8,128)S(1)} custom-call(f32[1,128,128]{2,1,0:T(8,128)S(1)} %get-tuple-element.54), custom_call_target="InvertDiagBlocksLowerTriangular" | custom-call | tf_op jit(solution)/shard_map/jit(cholesky)/cholesky | solution.py:58
  561.6 11.7 %cholesky.398 = f32[128,128]{1,0:T(8,128)S(1)} custom-call(f32[128,128]{1,0:T(8,128)S(1)} %cholesky.448), custom_call_target="Cholesky" | custom-call | tf_op jit(solution)/shard_map/jit(cholesky)/cholesky | solution.py:58
  574.0 9.8 %custom-call.33 = f32[1,128,128]{1,2,0:T(8,128)S(1)} custom-call(f32[1,128,128]{2,1,0:T(8,128)S(1)} %get-tuple-element.51), custom_call_target="InvertDiagBlocksLowerTriangular" | custom-call | tf_op jit(solution)/shard_map/jit(cholesky)/cholesky | solution.py:58
  584.4 11.7 %cholesky.415 = f32[128,128]{1,0:T(8,128)S(1)} custom-call(f32[128,128]{1,0:T(8,128)S(1)} %convolution_subtract_fusion.8), custom_call_target="Cholesky" | custom-call | tf_op jit(solution)/shard_map/jit(cholesky)/cholesky | solution.py:58
  599.7 7.7 while.5
  600.3 1.3 bitcast_dynamic-update-slice_fusion.5
  602.3 1.3 bitcast_dynamic-update-slice_fusion.5
  604.2 1.3 bitcast_dynamic-update-slice_fusion.5
  606.1 1.3 bitcast_dynamic-update-slice_fusion.5
  607.4 39.3 %custom-call.34 = f32[4,128,128]{1,2,0:T(8,128)S(1)} custom-call(f32[4,128,128]{2,1,0:T(8,128)S(1)} %get-tuple-element.19), custom_call_target="InvertDiagBlocksLowerTriangular" | custom-call | tf_op jit(solution)/shard_map/triangular_solve/custom-call.3 | solution.py:17
  646.8 2.4 fusion.37
  649.2 3.0 convolution_subtract_fusion.2
  653.3 3.5 convolution_subtract_fusion
  656.9 1.1 fusion.65
  658.0 5.6 fusion.21
  664.7 2.5 pad_maximum_fusion.2
  667.2 5.3 copy.26
  672.5 4.9 select_select_fusion
  677.5 103.0 %all-reduce.16.cloned.1.call-done = f32[4,512,512]{2,1,0:T(8,128)} async-done(((f32[4,512,512]{2,1,0:T(8,128)}), f32[4,512,512]{2,1,0:T(8,128)}) %all-reduce.16.cloned.1.call-update) | async-done | bytes 4194320 | tf_op jit(solution)/shard_map/psum | solution.py:11
  780.5 3.1 fusion.33
  783.7 8.3 pad_maximum_fusion
  792.1 57.1 %all-reduce.18.cloned.1.call-done = f32[2,512,512]{2,1,0:T(8,128)} async-done(((f32[2,512,512]{2,1,0:T(8,128)}), f32[2,512,512]{2,1,0:T(8,128)}) %all-reduce.18.cloned.1.call-update) | async-done | bytes 2097168 | tf_op jit(solution)/shard_map/psum | solution.py:11
  849.2 18.1 %multiply_multiply_fusion = f32[4,512,2,512]{1,3,2,0:T(8,128)} fusion(f32[4,512,2,512]{1,3,2,0:T(8,128)} %copy-done, f32[2]{0:T(128)S(1)} %compare_convert_fusion, f32[4]{0:T(128)S(1)} %compare_convert_fusion.1, f32[4,512,512]{2,1,0:T(8,128)} %all-reduce.16.cloned.1.call-done, f32[2,512,512]{2,1,0:T(8,128)} %all-reduce.18.cloned.1.call-done), kind=kOutput, calls=%fused_computation.5 | convolution fusion | flops 12891193344 | bytes 23068696 | tf_op jit(solution)/shard_map/mab,ncb->manc/dot_general | solution.py:26
  867.3 13.1 %copy.29 = f32[4,512,2,512]{3,2,1,0:T(2,128)} copy(f32[4,512,2,512]{1,3,2,0:T(8,128)} %multiply_multiply_fusion) | data formatting | bytes 16777216
  (99 shorter events, 23.5 us)
Async XLA Ops:
  7.2 88.3 %all-reduce.8.cloned.1.call-start = ((), (), s32[]{:S(2)}) async-start(), calls=%async_computation | async-start | bytes 2097152 | tf_op jit(solution)/shard_map/psum | solution.py:11
  25.9 3.4 copy-start.1
  30.4 331.5 %all-reduce.10.cloned.1.call-start = ((), (), s32[]{:S(2)}) async-start(), calls=%async_computation.1 | async-start | bytes 8388608 | tf_op jit(solution)/shard_map/psum | solution.py:11
  95.5 1.8 copy-start.4
  228.8 6.6 copy-start.2
  259.5 171.1 %all-reduce.12.cloned.1.call-start = ((), (), s32[]{:S(2)}) async-start(), calls=%async_computation.2 | async-start | bytes 4194304 | tf_op jit(solution)/shard_map/psum | solution.py:11
  365.1 149.0 %all-reduce.14.cloned.1.call-start = ((), (), s32[]{:S(2)}) async-start(), calls=%async_computation.3 | async-start | bytes 2097152 | tf_op jit(solution)/shard_map/psum | solution.py:11
  447.5 3.4 copy-start
  452.0 328.5 %all-reduce.16.cloned.1.call-start = ((), (), s32[]{:S(2)}) async-start(), calls=%async_computation.4 | async-start | bytes 8388608 | tf_op jit(solution)/shard_map/psum | solution.py:11
  514.1 1.2 copy-start.5
  646.8 6.6 copy-start.3
  677.5 171.7 %all-reduce.18.cloned.1.call-start = ((), (), s32[]{:S(2)}) async-start(), calls=%async_computation.5 | async-start | bytes 4194304 | tf_op jit(solution)/shard_map/psum | solution.py:11
Sparse Core Ops, SparseCore 0:
  30.5 64.9 all-reduce.7
  259.6 102.3 all-reduce.9
  365.2 65.3 all-reduce.11
  452.1 61.9 all-reduce.13
  677.6 102.8 all-reduce.15
  783.8 65.3 all-reduce.17
where the time goes:
time: 892 us; the launch traced here: 888 us
  waiting for transfers between devices  435 us (49%)
  other arithmetic  276 us (31%)
  local copies, waits for them, and re-layouts  81.6 us (9%)
  matrix products  74.4 us (8%)
  between operations  20.1 us (2%)
    psum x6, waiting for transfers between devices, from_root(): return lax.psum(jnp.where(mine, value, jnp.zeros_like(value)), axis)  435 us
    another operation x29, other arithmetic, make_panel(): factor = jnp.linalg.cholesky(diagonal)  158 us
    another operation x7, other arithmetic, solve_below(): lax.linalg.triangular_solve(factor, rhs_block, left_side=True, lower=True)  84.2 us
    another operation x14, matrix products, solve_below(): lax.linalg.triangular_solve(factor, rhs_block, left_side=True, lower=True)  35.6 us
    dot_general x2, matrix products, outer_update(): jnp.einsum('mab,ncb->manc', row_part, col_part, precision=lax.Precision.H...  35 us
    unnamed x14, local copies, waits for them, and re-layouts  33.8 us
    another operation x28, local copies, waits for them, and re-layouts, solve_below(): lax.linalg.triangular_solve(factor, rhs_block, left_side=True, lower=True)  20.8 us
    transpose x4, local copies, waits for them, and re-layouts, solve_below(): rhs_block = jnp.transpose(column, (2, 0, 1)).reshape(TILE, count * TILE)  20.4 us
  transfers between devices with their start and end apart: 6, of which 6 were waited for; matrix products, arithmetic and copies ran while one was open for 3% of the time, Pallas kernels for 0%

commit v1 on v0

--- a/solution.py
+++ b/solution.py
@@ -8,7 +8,10 @@
 
 def from_root(value, axis, root):
     mine = lax.axis_index(axis) == root
-    return lax.psum(jnp.where(mine, value, jnp.zeros_like(value)), axis)
+    begin_the_edges = lambda incoming_x, ax_name: lax.all_gather(incoming_x, axis_name=ax_name).sum(
+        axis=0
+    )
+    return begin_the_edges(jnp.where(mine, value, jnp.zeros_like(value)), axis)
 
 
 def solve_below(factor, column, tile_ids, index):

time: 892 us -> 1550 us (1.74)
  waiting for transfers between devices: 435 us -> 970 us
  other arithmetic: 276 us -> 360 us
  matrix products: 74.4 us -> 99.2 us
    all_gather x0 -> x6, waiting for transfers between devices: none -> 970 us  [from_root(): lax.all_gather(incoming_x, axis_name=ax_name).sum(axis=0)]
    psum x6 -> x0, waiting for transfers between devices: 435 us -> none  [from_root(): return lax.psum(jnp.where(mine, value, jnp.zeros_like(value)), axis)]
    reduce_sum x0 -> x6, other arithmetic: none -> 71.4 us  [from_root(): lax.all_gather(incoming_x, axis_name=ax_name).sum(axis=0)]
    dot_general x2, matrix products: 35 us -> 59.7 us  [outer_update(): jnp.einsum('mab,ncb->manc', row_part, col_part, precision=lax.Precision.H...]
    transpose x4 -> x0, local copies, waits for them, and re-layouts: 20.4 us -> none  [solve_below(): rhs_block = jnp.transpose(column, (2, 0, 1)).reshape(TILE, count * TILE)]
    unnamed x14 -> x12, local copies, waits for them, and re-layouts: 33.8 us -> 44.6 us
where the time goes in v1:
time: 1550 us; the launch traced here: 1530 us
  waiting for transfers between devices  970 us (63%)
  other arithmetic  360 us (23%)
  matrix products  99.2 us (6%)
  local copies, waits for them, and re-layouts  82.7 us (5%)
  between operations  20.2 us (1%)
    all_gather x6, waiting for transfers between devices, from_root(): lax.all_gather(incoming_x, axis_name=ax_name).sum(axis=0)  970 us
    another operation x29, other arithmetic, make_panel(): factor = jnp.linalg.cholesky(diagonal)  170 us
    another operation x7, other arithmetic, solve_below(): lax.linalg.triangular_solve(factor, rhs_block, left_side=True, lower=True)  84.2 us
    reduce_sum x6, other arithmetic, from_root(): lax.all_gather(incoming_x, axis_name=ax_name).sum(axis=0)  71.4 us
    dot_general x2, matrix products, outer_update(): jnp.einsum('mab,ncb->manc', row_part, col_part, precision=lax.Precision.H...  59.7 us
    unnamed x12, local copies, waits for them, and re-layouts  44.6 us
    another operation x14, matrix products, solve_below(): lax.linalg.triangular_solve(factor, rhs_block, left_side=True, lower=True)  35.8 us
  transfers between devices with their start and end apart: 6, of which 6 were waited for; matrix products, arithmetic and copies ran while one was open for 3% of the time, Pallas kernels for 0%

profile of v1, /device:TPU:0, one launch (start us, length us, event | category | flops | bytes accessed | tf_op | source)
XLA Modules:
  0.0 1533.1 jit_solution(17597565671001925369)
XLA Ops:
  8.3 5.0 copy_multiply_fusion
  13.3 3.4 copy-done
  17.9 4.6 slice.159
  22.6 47.6 %all-gather.13.cloned.1.call-done = f32[8,512,1,512]{3,1,2,0:T(8,128)} async-done(((f32[1,512,1,512]{3,1,2,0:T(8,128)}), f32[8,512,1,512]{3,1,2,0:T(8,128)}) %all-gather.13.cloned.1.call-update) | async-done | bytes 8388624 | tf_op jit(solution)/shard_map/all_gather | solution.py:11
  70.2 4.5 reduce_sum.54
  75.8 11.7 cholesky.286
  87.5 9.8 custom-call.27
  98.2 11.9 cholesky.305
  110.1 9.8 custom-call.28
  120.6 11.7 cholesky.326
  133.1 9.8 custom-call.29
  143.5 23.2 %cholesky.343 = f32[128,128]{1,0:T(8,128)S(1)} custom-call(f32[128,128]{1,0:T(8,128)S(1)} %convolution_subtract_fusion.9), custom_call_target="Cholesky" | custom-call | tf_op jit(solution)/shard_map/jit(cholesky)/cholesky | solution.py:61
  170.9 8.1 while.4
  171.6 1.3 bitcast_dynamic-update-slice_fusion.4
  173.7 1.3 bitcast_dynamic-update-slice_fusion.4
  175.7 1.3 bitcast_dynamic-update-slice_fusion.4
  177.7 1.3 bitcast_dynamic-update-slice_fusion.4
  179.1 39.3 %custom-call.30 = f32[4,128,128]{1,2,0:T(8,128)S(1)} custom-call(f32[4,128,128]{2,1,0:T(8,128)S(1)} %get-tuple-element.18), custom_call_target="InvertDiagBlocksLowerTriangular" | custom-call | tf_op jit(solution)/shard_map/triangular_solve/custom-call.3 | solution.py:20
  218.4 2.4 fusion.37
  220.9 3.0 convolution_subtract_fusion.3
  225.0 3.5 convolution_subtract_fusion.1
  229.6 5.7 fusion.24
  236.5 2.5 pad_maximum_fusion.1
  239.0 5.3 copy.33
  244.3 4.9 select_select_fusion.1
  249.4 369.0 %all-gather.15.cloned.1.call-done = f32[64,512,512]{2,1,0:T(8,128)} async-done(((f32[4,512,512]{2,1,0:T(8,128)}), f32[64,512,512]{2,1,0:T(8,128)}) %all-gather.15.cloned.1.call-update) | async-done | bytes 67108880 | tf_op jit(solution)/shard_map/all_gather | solution.py:11
  618.4 23.1 %reduce_sum.55 = f32[4,512,512]{2,1,0:T(8,128)} reduce(f32[16,4,512,512]{3,2,1,0:T(8,128)} %bitcast.20, f32[]{:T(128)} %constant.163.clone.1), dimensions={0}, to_apply=%region_9.12 | reduce | flops 15728640 | bytes 71303168 | tf_op jit(solution)/shard_map/reduce_sum | solution.py:11
  641.5 3.2 dynamic-slice_select_fusion.1
  644.7 5.4 copy.41
  650.2 79.2 %all-gather.17.cloned.1.call-done = f32[16,1,512,512]{3,2,1,0:T(8,128)} async-done(((f32[2,1,512,512]{3,2,1,0:T(8,128)}), f32[16,1,512,512]{3,2,1,0:T(8,128)}) %all-gather.17.cloned.1.call-update) | async-done | bytes 16777232 | tf_op jit(solution)/shard_map/all_gather | solution.py:11
  729.4 8.1 bitcast_reduce_fusion.1
  737.5 29.5 %fusion.18 = f32[4,512,2,512]{3,1,2,0:T(8,128)S(1)} fusion(f32[4,512,2,512]{3,1,2,0:T(8,128)} %copy-done, f32[4,512,512,1]{1,0,2,3:T(4,128)} %bitcast.136, f32[2,512,512]{2,1,0:T(8,128)S(1)} %bitcast_reduce_fusion.1), kind=kOutput, calls=%fused_computation.29 | convolution fusion | flops 12886999040 | bytes 23068672 | tf_op jit(solution)/shard_map/mab,ncb->manc/dot_general | solution.py:29
  767.0 3.4 copy-done.1
  771.8 4.6 slice.172
  776.5 45.6 %all-gather.19.cloned.1.call-done = f32[8,512,1,512]{3,1,2,0:T(8,128)} async-done(((f32[1,512,1,512]{3,1,2,0:T(8,128)}), f32[8,512,1,512]{3,1,2,0:T(8,128)}) %all-gather.19.cloned.1.call-update) | async-done | bytes 8388624 | tf_op jit(solution)/shard_map/all_gather | solution.py:11
  822.1 4.5 reduce_sum.57
  827.6 11.7 cholesky.358
  839.5 9.8 custom-call.31
  850.0 12.1 cholesky.377
  863.5 9.8 custom-call.32
  873.9 11.7 cholesky.398
  886.3 9.8 custom-call.33
  896.8 11.9 cholesky.415
  912.2 8.1 while.5
  912.9 1.3 bitcast_dynamic-update-slice_fusion.5
  914.9 1.3 bitcast_dynamic-update-slice_fusion.5
  920.3 39.3 %custom-call.34 = f32[4,128,128]{1,2,0:T(8,128)S(1)} custom-call(f32[4,128,128]{2,1,0:T(8,128)S(1)} %get-tuple-element.19), custom_call_target="InvertDiagBlocksLowerTriangular" | custom-call | tf_op jit(solution)/shard_map/triangular_solve/custom-call.3 | solution.py:20
  959.7 2.4 fusion.35
  962.1 3.0 convolution_subtract_fusion.2
  966.2 3.5 convolution_subtract_fusion
  970.9 5.6 fusion.21
  977.5 2.5 pad_maximum_fusion.2
  980.0 5.3 copy.37
  985.4 4.9 select_select_fusion
  990.4 369.0 %all-gather.21.cloned.1.call-done = f32[64,512,512]{2,1,0:T(8,128)} async-done(((f32[4,512,512]{2,1,0:T(8,128)}), f32[64,512,512]{2,1,0:T(8,128)}) %all-gather.21.cloned.1.call-update) | async-done | bytes 67108880 | tf_op jit(solution)/shard_map/all_gather | solution.py:11
  1359.4 23.1 %reduce_sum.58 = f32[4,512,512]{2,1,0:T(8,128)} reduce(f32[16,4,512,512]{3,2,1,0:T(8,128)} %bitcast.43, f32[]{:T(128)} %constant.163.clone.1), dimensions={0}, to_apply=%region_12.15 | reduce | flops 15728640 | bytes 71303168 | tf_op jit(solution)/shard_map/reduce_sum | solution.py:11
  1382.5 3.2 dynamic-slice_select_fusion
  1385.8 5.4 copy.42
  1391.2 9.9 pad_maximum_fusion
  1401.1 9.9 copy.30
  1411.0 59.4 %all-gather.23.cloned.1.call-done = f32[16,1,512,512]{3,2,1,0:T(8,128)} async-done(((f32[2,1,512,512]{3,2,1,0:T(8,128)}), f32[16,1,512,512]{3,2,1,0:T(8,128)}) %all-gather.23.cloned.1.call-update) | async-done | bytes 16777232 | tf_op jit(solution)/shard_map/all_gather | solution.py:11
  1470.5 8.1 bitcast_reduce_fusion
  1478.6 30.3 %multiply_multiply_fusion = f32[4,512,2,512]{3,1,2,0:T(8,128)S(1)} fusion(f32[4,512,2,512]{3,1,2,0:T(8,128)} %copy-done.1, f32[2]{0:T(128)S(1)} %compare_convert_fusion, f32[4]{0:T(128)S(1)} %compare_convert_fusion.1, f32[4,512,512,1]{1,0,2,3:T(4,128)} %bitcast.137, f32[2,512,512]{2,1,0:T(8,128)S(1)} %bitcast_reduce_fusion), kind=kOutput, calls=%fused_computation.8 | convolution fusion | flops 12891193344 | bytes 23068696 | tf_op jit(solution)/shard_map/mab,ncb->manc/dot_general | solution.py:29
  1508.8 17.0 %copy.29 = f32[4,512,2,512]{3,2,1,0:T(2,128)} copy(f32[4,512,2,512]{3,1,2,0:T(8,128)S(1)} %multiply_multiply_fusion) | data formatting | bytes 16777216
  (103 shorter events, 30.2 us)
Async XLA Ops:
  7.2 63.1 %all-gather.13.cloned.1.call-start = ((), (), s32[]{:S(2)}) async-start(), calls=%async_computation | async-start | bytes 9437184 | tf_op jit(solution)/shard_map/all_gather | solution.py:11
  13.3 3.4 copy-start
  17.9 600.5 %all-gather.15.cloned.1.call-start = ((), (), s32[]{:S(2)}) async-start(), calls=%async_computation.1 | async-start | bytes 71303168 | tf_op jit(solution)/shard_map/all_gather | solution.py:11
  218.4 6.6 copy-start.2
  249.3 480.1 %all-gather.17.cloned.1.call-start = ((), (), s32[]{:S(2)}) async-start(), calls=%async_computation.2 | async-start | bytes 18874368 | tf_op jit(solution)/shard_map/all_gather | solution.py:11
  644.7 177.4 %all-gather.19.cloned.1.call-start = ((), (), s32[]{:S(2)}) async-start(), calls=%async_computation.3 | async-start | bytes 9437184 | tf_op jit(solution)/shard_map/all_gather | solution.py:11
  767.0 3.4 copy-start.1
  771.6 587.8 %all-gather.21.cloned.1.call-start = ((), (), s32[]{:S(2)}) async-start(), calls=%async_computation.4 | async-start | bytes 71303168 | tf_op jit(solution)/shard_map/all_gather | solution.py:11
  959.7 6.6 copy-start.3
  990.3 480.1 %all-gather.23.cloned.1.call-start = ((), (), s32[]{:S(2)}) async-start(), calls=%async_computation.5 | async-start | bytes 18874368 | tf_op jit(solution)/shard_map/all_gather | solution.py:11
Sparse Core Ops, SparseCore 0:
  18.0 52.1 all-gather.12
  249.4 368.9 all-gather.14
  644.8 84.5 all-gather.16
  771.7 50.2 all-gather.18
  990.4 368.9 all-gather.20
  1385.9 84.5 all-gather.22
